TPU v7x, 256 devices: a whole 4x4x8 slice. The times are simulated.
256 devices in a mesh: expert: 16 (over z, core), token: 16 (over y, x).
Axes of the slice: x: 4, y: 4, z: 8, core: 2. Of those that a mesh axis runs over, the one named last changes fastest.
Arguments:
- tokens: bfloat16 [32768, 7168], P(('expert', 'token')), may hold values from -6 to 6
- routes: int32 [32768, 2], P(('expert', 'token')), may hold values from 0 to 15, all different within a row; in each aligned block of 128 rows (0 to 127, 128 to 255, ...) at most 32 rows name the same one
- owner_of: int32 [16], replicated, may hold values from 0 to 15, each once
- weights: bfloat16 [16, 2048, 7168], P('expert', 'token'), may hold values from -6 to 6
- hinv_diag: float32 [16, 128], P('expert'), may hold values from 0.5 to 2
- hinv_rows: float32 [16, 128, 7168], P('expert'), may hold values from -1 to 1
Outputs:
- gram: float32 [16, 7168, 128], P('expert', 'token')
- updated: bfloat16 [16, 2048, 7168], P('expert', 'token')
Inputs may be any that keep to these rules, and one draw needn't show every extreme that they name: `routes`: among the tokens of one device (aligned blocks of 128 rows), no expert is named by more than 32 tokens, a bound that some block reaches; a token's experts are distinct. `owner_of`: each slot holds exactly one expert.
All inputs are finite; a program needn't handle non-finite values.
Results may differ from a plain program's by a relative error of at most 0.005.
Values may be sent and summed in bfloat16 or wider, within the bound.
A program may use at most 128 MiB of HBM per device.

v0:
```python
import math

import jax
import jax.numpy as jnp
from jax import lax
from jax.sharding import PartitionSpec as P

PANEL = 128
TOP = 2
CAP = 32


def round_panel(weight_rows, colfac, diag_block, factor_rows):
    work = weight_rows.astype(jnp.float32)
    panel = work[:, :PANEL]
    step = jnp.max(jnp.abs(panel), axis=1) / 7.0 + 1e-06
    steps_grid = step[:, None] * colfac[None, :]
    column_ids = jnp.arange(PANEL)
    errors = jnp.zeros_like(panel)

    def advance(j, carry):
        panel, errors = carry
        value = lax.dynamic_slice_in_dim(panel, j, 1, 1)[:, 0]
        width = lax.dynamic_slice_in_dim(steps_grid, j, 1, 1)[:, 0]
        rounded = value - width / (2.0 * math.pi) * jnp.sin(2.0 * math.pi * value / width)
        fault = (value - rounded) / diag_block[j]
        row = lax.dynamic_slice_in_dim(factor_rows, j, 1, 0)[0, :PANEL]
        row = jnp.where(column_ids > j, row, 0.0)
        panel = panel - fault[:, None] * row[None, :]
        panel = jnp.where(column_ids[None, :] == j, rounded[:, None], panel)
        errors = jnp.where(column_ids[None, :] == j, fault[:, None], errors)
        return (panel, errors)

    panel, errors = lax.fori_loop(0, PANEL, advance, (panel, errors))
    rest = work[:, PANEL:] - jnp.dot(
        errors, factor_rows[:, PANEL:], precision=lax.Precision.HIGHEST
    )
    return jnp.concatenate([panel, rest], axis=1).astype(jnp.bfloat16)


def body(tokens, routes, owner_of, weights, hinv_diag, hinv_rows):
    owners = lax.axis_size("expert")
    shards = lax.axis_size("token")
    tok_rows = tokens.shape[0]
    width = tokens.shape[1]
    scale = owners / (tok_rows * owners * shards * TOP)
    flat = routes.reshape(-1)
    pair_token = jnp.repeat(jnp.arange(tok_rows, dtype=jnp.int32), TOP)
    onehot = (flat[:, None] == jnp.arange(owners, dtype=jnp.int32)[None, :]).astype(jnp.int32)
    before = jnp.cumsum(onehot, axis=0) - onehot
    position = jnp.sum(before * onehot, axis=1)
    target = jnp.sum(onehot * owner_of[None, :], axis=1)
    slot_of_pair = target * CAP + position
    slot_ids = jnp.arange(owners * CAP, dtype=jnp.int32)
    match = slot_of_pair[None, :] == slot_ids[:, None]
    source = jnp.sum(jnp.where(match, pair_token[None, :], 0), axis=1)
    filled = jnp.any(match, axis=1)
    send = jnp.where(filled[:, None], tokens[source], jnp.zeros((), jnp.bfloat16))
    send = send.reshape(owners, CAP, width)
    share = width // shards
    arrived = lax.all_to_all(send, "expert", split_axis=0, concat_axis=0, tiled=True).reshape(
        owners * CAP, width
    )
    panel_rows = arrived[:, :PANEL]
    partial_sum = (
        jnp.einsum("rd,rp->dp", arrived, panel_rows, preferred_element_type=jnp.float32) * scale
    )
    total = lax.psum(partial_sum, "token")
    piece = lax.dynamic_slice_in_dim(total, lax.axis_index("token") * share, share, 0)
    dgram = jnp.diagonal(total[:PANEL, :])
    colfac = jnp.sqrt(jnp.mean(dgram) / (dgram + 1e-05))
    updated = round_panel(weights[0], colfac, hinv_diag[0], hinv_rows[0])
    return (piece[None], updated[None])


def solution(mesh):
    in_specs = (
        P(("expert", "token"), None),
        P(("expert", "token"), None),
        P(),
        P("expert", "token", None),
        P("expert", None),
        P("expert", None, None),
    )
    out_specs = (P("expert", "token", None), P("expert", "token", None))
    return jax.shard_map(body, mesh=mesh, in_specs=in_specs, out_specs=out_specs, check_vma=False)
```

profile of v0, /device:TPU:8, one launch (start us, length us, event | category | flops | bytes accessed | tf_op | source)
XLA Modules:
  0.0 597.8 jit_solution(4471225041505295123)
XLA Ops:
  7.2 0.9 copy.15
  9.4 0.7 select_reduce_fusion.1
  10.6 7.0 %gather_fusion = bf16[512,7168]{1,0:T(8,128)(2,1)} fusion(bf16[128,7168]{1,0:T(8,128)(2,1)S(1)} %copy-done, s32[1024]{0:T(1024)S(1)} %pad_clamp_fusion), kind=kCustom, calls=%fused_computation | custom fusion | bytes 14682112 | tf_op jit(solution)/shard_map/gather | solution.py:58
  17.6 3.6 broadcast_select_fusion
  21.3 170.5 %all_to_all.5 = bf16[16,32,7168]{2,1,0:T(8,128)(2,1)S(1)} all-to-all(bf16[16,32,7168]{2,1,0:T(8,128)(2,1)S(1)} %broadcast_select_fusion), channel_id=1, replica_groups=mesh['expert'=16,'token'=16] {'expert'}, dimensions={0} | all-to-all | bytes 14680064 | tf_op jit(solution)/shard_map/all_to_all | solution.py:61
  191.7 4.0 convolution_multiply_fusion
  195.7 1.9 bitcast_convert_fusion
  197.6 1.9 copy-done.1
  199.7 103.2 %all-reduce.2.cloned.1.call-done = f32[7168,128]{1,0:T(8,128)} async-done(((f32[7168,128]{1,0:T(8,128)}), f32[7168,128]{1,0:T(8,128)}) %all-reduce.2.cloned.1.call-update) | async-done | bytes 3670032 | tf_op jit(solution)/shard_map/psum | solution.py:68
  303.0 0.8 slice.44
  303.8 1.2 gather_fusion.1
  306.4 272.2 %while.17 = (s32[]{:T(128)}, f32[128,128]{0,1:T(8,128)S(1)}, f32[128,128]{0,1:T(8,128)S(1)}, f32[128,128]{0,1:T(8,128)S(1)}, f32[128]{0:T(128)S(1)}, /*index=5*/f32[128,7168]{1,0:T(8,128)}, s32[]{:T(128)}, s32[]{:T(128)}) while((s32[]{:T(128)}, f32[128,128]{0,1:T(8,128)S(1)}, f32[128,128]{0,1:T(8,128)S(1)}, ...), condition=%wide.region_10.11_spmd.clone.clone, body=%wide.region_9.10_spmd.clone.clone.sunk | while | flops 83203 | bytes 268151 | solution.py:34
  307.8 0.7 fusion.15
  309.9 0.7 fusion.15
  312.0 0.7 fusion.15
  326.9 0.7 fusion.15
  329.0 0.7 fusion.15
  331.1 0.7 fusion.15
  346.0 0.7 fusion.15
  348.2 0.7 fusion.15
  350.3 0.7 fusion.15
  352.4 0.7 fusion.15
  367.3 0.7 fusion.15
  369.4 0.7 fusion.15
  371.6 0.7 fusion.15
  386.4 0.7 fusion.15
  388.6 0.7 fusion.15
  390.7 0.7 fusion.15
  392.8 0.7 fusion.15
  578.7 7.7 %fusion.4 = bf16[1,128,7040]{2,1,0:T(8,128)(2,1)} fusion(f32[128,128]{0,1:T(8,128)S(1)} %get-tuple-element.131, f32[128,7168]{1,0:T(8,128)} %get-tuple-element.285, f32[128,7168]{1,0:T(8,128)} %copy-done.1), kind=kOutput, calls=%fused_computation.17 | convolution fusion | flops 1385922560 | bytes 9076736 | tf_op jit(solution)/shard_map/dot_general | solution.py:35
  586.5 2.9 pad_maximum_fusion
  589.3 1.6 dynamic-slice_bitcast_fusion
  (653 shorter events, 259.3 us)
Async XLA Ops:
  7.2 3.4 copy-start
  7.2 295.8 %all-reduce.2.cloned.1.call-start = ((), (), s32[]{:S(2)}) async-start(), calls=%async_computation.1 | async-start | bytes 7340032 | tf_op jit(solution)/shard_map/psum | solution.py:68
  195.7 110.7 %copy-start.2 = (f32[1,128]{1,0:T(1,128)S(1)}, f32[1,128]{1,0:T(1,128)}, u32[]{:S(2)}) copy-start(f32[1,128]{1,0:T(1,128)} %param.12) | copy-start | bytes 1540
  197.6 1.9 copy-start.1
Sparse Core Ops, SparseCore 0:
  195.8 107.0 all-reduce.1
where the time goes:
time: 605 us; the launch traced here: 598 us
  other arithmetic  204 us (34%)
  blocking collectives  170 us (28%)
  waiting for transfers between devices  103 us (17%)
  local copies, waits for them, and re-layouts  89.5 us (15%)
  between operations  14.8 us (2%)
  matrix products  11.7 us (2%)
    mul x256, other arithmetic, advance(): panel = panel - fault[:, None] * row[None, :]  179 us
    all_to_all x1, blocking collectives, body(): lax.all_to_all(send, 'expert', split_axis=0, concat_axis=0, tiled=True)  170 us
    psum x1, waiting for transfers between devices, body(): total = lax.psum(partial_sum, 'token')  103 us
    dynamic_slice x128, local copies, waits for them, and re-layouts, advance(): fault = (value - rounded) / diag_block[j]  75 us
    select_n x128, other arithmetic, advance(): errors = jnp.where(column_ids[None, :] == j, fault[:, None], errors)  13.9 us
  transfers between devices with their start and end apart: 1, of which 1 were waited for; matrix products, arithmetic and copies ran while one was open for 0% of the time, Pallas kernels for 0%

commit v1 on v0

v1 whole, which is shorter than its diff:
```python
import math

import jax
import jax.numpy as jnp
from jax import lax
from jax.experimental import pallas as pl
from jax.experimental.pallas import tpu as pltpu
from jax.sharding import PartitionSpec as P

D = 7168
PANEL = 128
TOP = 2
TOK = 128
SLOTS = 16
RING = 8
PLANE = 16
SHARE = 448
MSG = PANEL + SLOTS
MESH = pl.DeviceIdType.MESH
BF16 = jnp.bfloat16
F32 = jnp.float32
SCALE = 16.0 / 65536.0

SINE = (
    6.2831852700170625,
    -16.20895564378196,
    16.769189671870134,
    -9.624604702175908,
    3.5163760294927235,
    -0.7983429889808796,
)


def sine_of_turns(turns):
    r = turns - jnp.round(turns)
    y = r * r
    y2 = y * y
    low = SINE[0] + SINE[1] * y
    mid = SINE[2] + SINE[3] * y
    top = SINE[4] + SINE[5] * y
    edge = r - 4.0 * (r * y)
    return edge * (low + y2 * (mid + y2 * top))


def place_of(x):
    return jnp.where(x == 0, 0, jnp.where(x == 3, 1, x + 1))


def kernel(
    tokens,
    routes,
    owner,
    weights,
    hdiag,
    hrows,
    gram,
    updated,
    x0,
    msg,
    w_v,
    h_v,
    out_v,
    dg_own,
    dg_in,
    dg_mid,
    dg_fin,
    mt,
    x_left,
    x_two,
    x_one,
    ht,
    rot,
    work,
    inv,
    amp,
    dinv,
    errs,
    sib_out,
    sib_in,
    own,
    z_out,
    z_in,
    fin,
    left,
    left_out,
    left_in,
    local_sem,
    dg_s,
    dg_r,
    dgz_s,
    dgz_r,
    pa_s,
    pa_r,
    pb_s,
    pb_r,
    xl_s,
    xl_r,
    x2_s,
    x2_r,
    x1_s,
    x1_r,
    sib_s,
    sib_r,
    z_s,
    z_r,
    lx_s,
    lx_r,
):
    e = lax.axis_index("expert")
    t = lax.axis_index("token")
    z, c = e // 2, e % 2
    y, x = t // 4, t % 4
    u = 4 * place_of(x) + y
    group = u // 8
    side = x % 2

    def plane_peer(k):
        py, px = (y + k // 4) % 4, (x + k % 4) % 4
        return py, px, 4 * place_of(px) + py

    def z_peer(i):
        dz = jnp.where(i % 2 == 1, 4 - (i + 1) // 2, 4 + i // 2)
        return (z + dz) % RING

    def main_lane(py, px):
        return pl.multiple_of((7 * (2 * py + px // 2) + 4 * (px % 2)) * 128, 128)

    def left_lane(py, m):
        return pl.multiple_of((7 * (2 * py + m) + 3) * 128, 128)

    def left_x(m):
        inner = jnp.where(group == 1, 1, 0)
        return jnp.where(m == 0, inner, 3 - inner)

    def remote(src, dst, send, recv, device):
        return pltpu.make_async_remote_copy(
            src_ref=src,
            dst_ref=dst,
            send_sem=send,
            recv_sem=recv,
            device_id=device,
            device_id_type=MESH,
        )

    barrier = pltpu.get_barrier_semaphore()

    @pl.loop(1, 16)
    def _(k):
        py, px, _ = plane_peer(k)
        pl.semaphore_signal(barrier, inc=1, device_id=(e, 4 * py + px), device_id_type=MESH)

    @pl.loop(1, 16)
    def _(k):
        pl.semaphore_signal(barrier, inc=1, device_id=((e + k) % 16, t), device_id_type=MESH)

    get_x0 = pltpu.make_async_copy(tokens.at[:, pl.ds(0, 128)], x0, local_sem.at[0])
    get_w = pltpu.make_async_copy(weights, w_v, local_sem.at[1])
    get_h = pltpu.make_async_copy(hrows, h_v, local_sem.at[2])
    get_x0.start()
    get_w.start()
    get_h.start()

    first = jnp.broadcast_to(routes[:, 0:1].astype(F32), (TOK, 128)).T[0:SLOTS].astype(jnp.int32)
    second = jnp.broadcast_to(routes[:, 1:2].astype(F32), (TOK, 128)).T[0:SLOTS].astype(jnp.int32)
    slot_a = jnp.zeros((SLOTS, 128), jnp.int32)
    slot_b = jnp.zeros((SLOTS, 128), jnp.int32)
    for i in range(SLOTS):
        slot_a = jnp.where(first == i, owner[i], slot_a)
        slot_b = jnp.where(second == i, owner[i], slot_b)
    slot_row = lax.broadcasted_iota(jnp.int32, (SLOTS, 128), 0)
    mask = jnp.where((slot_a == slot_row) | (slot_b == slot_row), 1.0, 0.0).astype(F32)

    get_x0.wait()
    panel = x0[...].astype(F32)
    square = panel * panel
    high = square.astype(BF16)
    low = (square - high.astype(F32)).astype(BF16)
    mask16 = mask.astype(BF16)
    dg_own[...] = jnp.dot(mask16, high, preferred_element_type=F32) + jnp.dot(
        mask16, low, preferred_element_type=F32
    )
    msg[pl.ds(u, 1), pl.ds(0, PANEL), :] = panel.T.astype(BF16)[None]
    msg[pl.ds(u, 1), pl.ds(PANEL, SLOTS), :] = mask16[None]

    pl.semaphore_wait(barrier, 30)

    @pl.loop(1, 16)
    def _(k):
        py, px, _ = plane_peer(k)
        remote(dg_own, dg_in.at[u], dg_s.at[k], dg_r.at[u], (e, 4 * py + px)).start()

    dg_in[pl.ds(u, 1)] = dg_own[...][None]

    @pl.loop(1, 4)
    def _(k):
        remote(msg.at[u], msg.at[u], pa_s.at[k], pa_r.at[y], (e, 4 * ((y + k) % 4) + x)).start()

    own_rows = pl.ds(pl.multiple_of(u * TOK, TOK), TOK)
    left_rows = pl.ds(pl.multiple_of((u - 8 * group) * TOK, TOK), TOK)

    @pl.loop(0, 8)
    def _(k):
        py, m = (y + k // 2) % 4, k % 2
        px = left_x(m)
        src = tokens.at[:, pl.ds(left_lane(py, m), 128)]
        itself = (py == y) & (px == x)

        @pl.when(jnp.logical_not(itself))
        def _():
            remote(src, x_left.at[left_rows], xl_s.at[k], xl_r.at[u - 8 * group], (e, 4 * py + px)).start()

        @pl.when(itself)
        def _():
            pltpu.make_async_copy(src, x_left.at[left_rows], local_sem.at[3]).start()

    keep_two = pltpu.make_async_copy(
        tokens.at[:, pl.ds(main_lane(y, x), 256)], x_two.at[own_rows], local_sem.at[4]
    )
    keep_one = pltpu.make_async_copy(
        tokens.at[:, pl.ds(main_lane(y, x) + 256, 128)], x_one.at[own_rows], local_sem.at[5]
    )
    keep_two.start()
    keep_one.start()

    @pl.loop(1, 4)
    def _(k):
        py = (y + k) % 4
        pu = 4 * (u // 4) + py
        remote(msg.at[pu], msg.at[pu], pa_s.at[k], pa_r.at[py], (e, 4 * py + x)).wait_recv()

    mine = pl.ds(4 * (u // 4), 4)

    @pl.loop(1, 4)
    def _(k):
        px = (x + k) % 4
        remote(msg.at[mine], msg.at[mine], pb_s.at[k], pb_r.at[x], (e, 4 * y + px)).start()

    @pl.loop(1, 16)
    def _(k):
        py, px, pu = plane_peer(k)
        src = tokens.at[:, pl.ds(main_lane(py, px), 256)]
        remote(src, x_two.at[own_rows], x2_s.at[k], x2_r.at[u], (e, 4 * py + px)).start()

    @pl.loop(1, 16)
    def _(k):
        py, px, pu = plane_peer(k)
        src = tokens.at[:, pl.ds(main_lane(py, px) + 256, 128)]
        remote(src, x_one.at[own_rows], x1_s.at[k], x1_r.at[u], (e, 4 * py + px)).start()

    @pl.loop(1, 16)
    def _(k):
        py, px, pu = plane_peer(k)
        remote(dg_own, dg_in.at[pu], dg_s.at[k], dg_r.at[pu], (e, 4 * py + px)).wait_recv()

    dg_mid[...] = jnp.sum(dg_in[...], axis=0)

    @pl.loop(1, 16)
    def _(k):
        pe = (e + k) % 16
        src = dg_mid.at[pl.ds(pl.multiple_of(8 * (pe // 8), 8), 8)]
        remote(src, dg_fin.at[e], dgz_s.at[k], dgz_r.at[e], (pe, t)).start()

    dg_fin[pl.ds(e, 1)] = dg_mid[pl.ds(pl.multiple_of(8 * (e // 8), 8), 8), :][None]

    get_w.wait()
    get_h.wait()
    wide = w_v[:, 0:PANEL].astype(F32).T
    work[...] = wide
    step = jnp.max(jnp.abs(wide), axis=0, keepdims=True) / 7.0 + 1e-06
    cols = lax.broadcasted_iota(jnp.int32, (PANEL, PANEL), 0)
    rows = lax.broadcasted_iota(jnp.int32, (PANEL, PANEL), 1)
    ht[...] = jnp.where(cols > rows, h_v[:, 0:PANEL].T, 0.0)
    dinv[...] = 1.0 / jnp.broadcast_to(hdiag[...], (PANEL, PANEL)).T

    @pl.loop(1, 16)
    def _(k):
        pe = (e + k) % 16
        src = dg_mid.at[pl.ds(pl.multiple_of(8 * (e // 8), 8), 8)]
        remote(src, dg_fin.at[pe], dgz_s.at[k], dgz_r.at[pe], (pe, t)).wait_recv()

    eight = jnp.sum(dg_fin[...], axis=0)
    this = lax.broadcasted_iota(jnp.int32, (8, 128), 0) == e % 8
    dgram = jnp.sum(jnp.where(this, eight, 0.0), axis=0, keepdims=True) * SCALE
    colfac = jnp.sqrt(jnp.mean(dgram, axis=1, keepdims=True) / (dgram + 1e-05))
    grid_step = jnp.broadcast_to(colfac, (PANEL, PANEL)).T * step
    amp[...] = grid_step / (2.0 * math.pi)
    inv[...] = 1.0 / grid_step

    def round_columns(b):
        j0 = pl.multiple_of(b * 8, 8)
        at = pl.ds(j0, 8)
        rot[...] = pltpu.roll(ht[...], (PANEL - b * 8) % PANEL, 1)
        near = rot[at, :]
        block = work[at, :]
        inv_b, amp_b, dinv_b = inv[at, :], amp[at, :], dinv[at, :]
        row = lax.broadcasted_iota(jnp.int32, (8, 128), 0)
        faults = []
        fault_rows = jnp.zeros((8, 128), F32)
        for j in range(8):
            value = jnp.broadcast_to(block[j : j + 1], (8, 128))
            turns = value * jnp.broadcast_to(inv_b[j : j + 1], (8, 128))
            moved = sine_of_turns(turns) * jnp.broadcast_to(amp_b[j : j + 1], (8, 128))
            fault = moved * jnp.broadcast_to(dinv_b[j : j + 1], (8, 128))
            coef = jnp.broadcast_to(near[:, j : j + 1], (8, 128))
            block = jnp.where(row == j, value - moved, block - fault * coef)
            fault_rows = jnp.where(row == j, fault, fault_rows)
            faults.append(fault)
        for k in range(16):
            part = pl.ds(8 * k, 8)
            acc = work[part, :]
            for j in range(8):
                acc = acc - faults[j] * jnp.broadcast_to(rot[part, j : j + 1], (8, 128))
            work[part, :] = acc
        work[at, :] = block
        errs[at, :] = fault_rows

    @pl.loop(0, 8)
    def _(b):
        round_columns(b)

    @pl.loop(1, 4)
    def _(k):
        px = (x + k) % 4
        theirs = pl.ds(4 * place_of(px), 4)
        remote(msg.at[theirs], msg.at[theirs], pb_s.at[k], pb_r.at[px], (e, 4 * y + px)).wait_recv()

    def mask_panels(half):
        for pu in range(8):
            sender = 8 * half + pu
            their = msg[sender, 0:PANEL, :]
            flags = msg[sender, PANEL:MSG, :]
            for s in range(SLOTS):
                side_row = jnp.where(c == s % 2, 1, 0)
                value = their * jnp.broadcast_to(flags[s : s + 1], (PANEL, TOK))
                mt[
                    half,
                    pl.ds(pl.multiple_of(side_row * 1024 + (s // 2) * PANEL, PANEL), PANEL),
                    pl.ds(pu * TOK, TOK),
                ] = value

    @pl.loop(0, 2)
    def _(half):
        mask_panels(half)

    def partial_rows(m, source, is_left):
        at = pl.ds(pl.multiple_of(m * 256, 256), 256)
        if is_left:
            return jnp.dot(mt[group, at, :], source[...], preferred_element_type=F32)
        return jnp.dot(mt[0, at, :], source[pl.ds(0, 1024), :], preferred_element_type=F32) + jnp.dot(
            mt[1, at, :], source[pl.ds(1024, 1024), :], preferred_element_type=F32
        )

    def grams(index, lane, width, source, is_left):
        lanes = pl.ds(lane, width)

        @pl.loop(0, 4)
        def _(m):
            at = pl.ds(pl.multiple_of(m * 256, 256), 256)
            sib_out[at, lanes] = partial_rows(m, source, is_left).astype(BF16)

        swap = remote(
            sib_out.at[:, lanes],
            sib_in.at[:, lanes],
            sib_s.at[index],
            sib_r.at[index],
            (2 * z + 1 - c, t),
        )
        swap.start()

        @pl.loop(0, 4)
        def _(m):
            at = pl.ds(pl.multiple_of(m * 256, 256), 256)
            own[at, lanes] = partial_rows(m + 4, source, is_left)

        swap.wait_recv()

        @pl.loop(0, 7)
        def _(i):
            pz = z_peer(i)
            at = pl.ds(pl.multiple_of(pz * PANEL, PANEL), PANEL)
            both = own[at, lanes] + sib_in[at, lanes].astype(F32)
            z_out[pl.ds(pz, 1), :, lanes] = both.astype(BF16)[None]
            remote(
                z_out.at[pz, :, lanes],
                z_in.at[z, :, lanes],
                z_s.at[index, i],
                z_r.at[index, z],
                (2 * pz + c, t),
            ).start()

        at = pl.ds(pl.multiple_of(z * PANEL, PANEL), PANEL)
        fin[:, lanes] = own[at, lanes] + sib_in[at, lanes].astype(F32)

    def gather_sum(index, lane, width):
        lanes = pl.ds(lane, width)

        @pl.loop(0, 7)
        def _(i):
            pz = z_peer(i)
            remote(
                z_out.at[pz, :, lanes],
                z_in.at[pz, :, lanes],
                z_s.at[index, i],
                z_r.at[index, pz],
                (2 * pz + c, t),
            ).wait_recv()
            fin[:, lanes] += z_in[pl.ds(pz, 1), :, lanes][0].astype(F32)

    @pl.loop(0, 8)
    def _(k):
        py, m = (y + k // 2) % 4, k % 2
        px = left_x(m)
        pu = 4 * place_of(px) + py - 8 * group
        theirs = pl.ds(pl.multiple_of(pu * TOK, TOK), TOK)
        src = tokens.at[:, pl.ds(left_lane(py, m), 128)]
        itself = (py == y) & (px == x)

        @pl.when(jnp.logical_not(itself))
        def _():
            remote(src, x_left.at[theirs], xl_s.at[k], xl_r.at[pu], (e, 4 * py + px)).wait_recv()

        @pl.when(itself)
        def _():
            pltpu.make_async_copy(src, x_left.at[theirs], local_sem.at[3]).wait()

    grams(0, 0, 128, x_left, True)

    @pl.loop(8, 16)
    def _(b):
        round_columns(b)

    keep_two.wait()

    @pl.loop(1, 16)
    def _(k):
        py, px, pu = plane_peer(k)
        src = tokens.at[:, pl.ds(main_lane(py, px), 256)]
        theirs = pl.ds(pl.multiple_of(pu * TOK, TOK), TOK)
        remote(src, x_two.at[theirs], x2_s.at[k], x2_r.at[pu], (e, 4 * py + px)).wait_recv()

    grams(1, 128, 256, x_two, False)

    err_rows = errs[...].T.astype(BF16)

    @pl.loop(0, 14)
    def _(i):
        lanes = pl.ds(pl.multiple_of(i * 512, 512), 512)
        fix = jnp.dot(err_rows, h_v[:, lanes].astype(BF16), preferred_element_type=F32)
        out_v[:, lanes] = (w_v[:, lanes].astype(F32) - fix).astype(BF16)

    out_v[:, 0:PANEL] = work[...].T.astype(BF16)
    put_out = pltpu.make_async_copy(out_v, updated, local_sem.at[6])
    put_out.start()

    gather_sum(0, 0, 128)
    left[...] = fin[:, 0:128].T * SCALE
    half_rows = pl.ds(pl.multiple_of((1 - side) * 64, 64), 64)
    left_out[...] = left[half_rows, :]
    swap_left = remote(left_out, left_in, lx_s.at[0], lx_r.at[0], (e, 4 * y + x + 1 - 2 * side))
    swap_left.start()

    keep_one.wait()

    @pl.loop(1, 16)
    def _(k):
        py, px, pu = plane_peer(k)
        src = tokens.at[:, pl.ds(main_lane(py, px) + 256, 128)]
        theirs = pl.ds(pl.multiple_of(pu * TOK, TOK), TOK)
        remote(src, x_one.at[theirs], x1_s.at[k], x1_r.at[pu], (e, 4 * py + px)).wait_recv()

    grams(2, 384, 128, x_one, False)

    base = 64 * side
    gather_sum(1, 128, 256)
    gram[pl.ds(pl.multiple_of(base, 64), 256), :] = fin[:, 128:384].T * SCALE
    swap_left.wait_recv()
    left_at = pl.ds(pl.multiple_of(384 * (1 - side), 64), 64)
    gram[left_at, :] = left[pl.ds(pl.multiple_of(side * 64, 64), 64), :] + left_in[...]
    gather_sum(2, 384, 128)
    gram[pl.ds(pl.multiple_of(base + 256, 64), 128), :] = fin[:, 384:512].T * SCALE

    @pl.loop(1, 16)
    def _(k):
        py, px, pu = plane_peer(k)
        to = (e, 4 * py + px)
        pe = (e + k) % 16
        remote(dg_own, dg_in.at[u], dg_s.at[k], dg_r.at[u], to).wait_send()
        src = dg_mid.at[pl.ds(pl.multiple_of(8 * (pe // 8), 8), 8)]
        remote(src, dg_fin.at[e], dgz_s.at[k], dgz_r.at[e], (pe, t)).wait_send()
        src = tokens.at[:, pl.ds(main_lane(py, px), 256)]
        remote(src, x_two.at[own_rows], x2_s.at[k], x2_r.at[u], to).wait_send()
        src = tokens.at[:, pl.ds(main_lane(py, px) + 256, 128)]
        remote(src, x_one.at[own_rows], x1_s.at[k], x1_r.at[u], to).wait_send()

    @pl.loop(1, 4)
    def _(k):
        to = (e, 4 * ((y + k) % 4) + x)
        remote(msg.at[u], msg.at[u], pa_s.at[k], pa_r.at[y], to).wait_send()
        to = (e, 4 * y + (x + k) % 4)
        remote(msg.at[mine], msg.at[mine], pb_s.at[k], pb_r.at[x], to).wait_send()

    @pl.loop(0, 8)
    def _(k):
        py, m = (y + k // 2) % 4, k % 2
        px = left_x(m)
        src = tokens.at[:, pl.ds(left_lane(py, m), 128)]

        @pl.when(jnp.logical_not((py == y) & (px == x)))
        def _():
            to = (e, 4 * py + px)
            remote(src, x_left.at[left_rows], xl_s.at[k], xl_r.at[u - 8 * group], to).wait_send()

    for index, lane, width in ((0, 0, 128), (1, 128, 256), (2, 384, 128)):
        lanes = pl.ds(lane, width)
        remote(
            sib_out.at[:, lanes],
            sib_in.at[:, lanes],
            sib_s.at[index],
            sib_r.at[index],
            (2 * z + 1 - c, t),
        ).wait_send()

        @pl.loop(0, 7)
        def _(i):
            pz = z_peer(i)
            remote(
                z_out.at[pz, :, lanes],
                z_in.at[z, :, lanes],
                z_s.at[index, i],
                z_r.at[index, z],
                (2 * pz + c, t),
            ).wait_send()

    swap_left.wait_send()
    put_out.wait()


def body(tokens, routes, owner_of, weights, hinv_diag, hinv_rows):
    vmem = pl.BlockSpec(memory_space=pltpu.VMEM)
    hbm = pl.BlockSpec(memory_space=pl.ANY)
    dma = pltpu.SemaphoreType.DMA
    square = pltpu.VMEM((PANEL, PANEL), F32)
    gram, updated = pl.pallas_call(
        kernel,
        out_shape=(
            jax.ShapeDtypeStruct((SHARE, PANEL), F32),
            jax.ShapeDtypeStruct((128, D), BF16),
        ),
        in_specs=[hbm, vmem, pl.BlockSpec(memory_space=pltpu.SMEM), hbm, vmem, hbm],
        out_specs=(vmem, hbm),
        scratch_shapes=[
            pltpu.VMEM((TOK, 128), BF16),
            pltpu.VMEM((PLANE, MSG, TOK), BF16),
            pltpu.VMEM((128, D), BF16),
            pltpu.VMEM((PANEL, D), F32),
            pltpu.VMEM((128, D), BF16),
            pltpu.VMEM((SLOTS, PANEL), F32),
            pltpu.VMEM((PLANE, SLOTS, PANEL), F32),
            pltpu.VMEM((SLOTS, PANEL), F32),
            pltpu.VMEM((16, 8, PANEL), F32),
            pltpu.VMEM((2, SLOTS * PANEL, 8 * TOK), BF16),
            pltpu.VMEM((8 * TOK, 128), BF16),
            pltpu.VMEM((PLANE * TOK, 256), BF16),
            pltpu.VMEM((PLANE * TOK, 128), BF16),
            square,
            square,
            square,
            square,
            square,
            square,
            square,
            pltpu.VMEM((RING * PANEL, 512), BF16),
            pltpu.VMEM((RING * PANEL, 512), BF16),
            pltpu.VMEM((RING * PANEL, 512), F32),
            pltpu.VMEM((RING, PANEL, 512), BF16),
            pltpu.VMEM((RING, PANEL, 512), BF16),
            pltpu.VMEM((PANEL, 512), F32),
            square,
            pltpu.VMEM((64, PANEL), F32),
            pltpu.VMEM((64, PANEL), F32),
            dma((8,)),
            dma((16,)),
            dma((16,)),
            dma((16,)),
            dma((16,)),
            dma((4,)),
            dma((4,)),
            dma((4,)),
            dma((4,)),
            dma((8,)),
            dma((8,)),
            dma((16,)),
            dma((16,)),
            dma((16,)),
            dma((16,)),
            dma((3,)),
            dma((3,)),
            dma((3, 7)),
            dma((3, 8)),
            dma((1,)),
            dma((1,)),
        ],
        compiler_params=pltpu.CompilerParams(
            collective_id=0, has_side_effects=True, vmem_limit_bytes=56 * 2**20
        ),
        cost_estimate=pl.CostEstimate(flops=4 * 10**9, bytes_accessed=10**7, transcendentals=0),
        name="calibrate",
    )(tokens, routes, owner_of, weights[0], hinv_diag, hinv_rows[0])
    return gram[None], updated[None]


def solution(mesh):
    in_specs = (
        P(("expert", "token"), None),
        P(("expert", "token"), None),
        P(),
        P("expert", "token", None),
        P("expert", None),
        P("expert", None, None),
    )
    out_specs = (P("expert", "token", None), P("expert", "token", None))
    return jax.shard_map(body, mesh=mesh, in_specs=in_specs, out_specs=out_specs, check_vma=False)
```

time: 605 us -> 73.2 us (0.12)
  other arithmetic: 204 us -> 0 us
  blocking collectives: 170 us -> 0 us
  waiting for transfers between devices: 103 us -> 0 us
  local copies, waits for them, and re-layouts: 89.5 us -> 5.9 us
  Pallas kernels: 0 us -> 65.4 us
  between operations: 14.8 us -> 0.64 us
  matrix products: 11.7 us -> 0 us
    mul x257 -> x0, other arithmetic: 179 us -> none  [the longest x256 179 us: advance(): panel = panel - fault[:, None] * row[None, :]]
    all_to_all x1 -> x0, blocking collectives: 170 us -> none  [body(): lax.all_to_all(send, 'expert', split_axis=0, concat_axis=0, tiled=True)]
    psum x1 -> x0, waiting for transfers between devices: 103 us -> none  [body(): total = lax.psum(partial_sum, 'token')]
    dynamic_slice x128 -> x0, local copies, waits for them, and re-layouts: 75 us -> none  [advance(): fault = (value - rounded) / diag_block[j]]
    pallas_call x0 -> x1, Pallas kernels: none -> 65.4 us  [body(): pl.pallas_call(kernel, out_shape=(jax.ShapeDtypeStruct((SHARE, PANEL), F3...]
    select_n x130 -> x0, other arithmetic: 17.6 us -> none  [the longest x128 13.9 us: advance(): errors = jnp.where(column_ids[None, :] == j, fault[:, None], errors)]
    dot_general x2 -> x0, matrix products: 11.7 us -> none  [the longest x1 7.69 us: round_panel(): jnp.dot(errors, factor_rows[:, PANEL:], precision=lax.Precision.HIGHEST)]
    gather x2 -> x0, local copies, waits for them, and re-layouts: 8.29 us -> none  [the longest x1 7.05 us: body(): tokens[source]]
  transfers between devices with their start and end apart: 1 -> 0, of which waited for: 1 -> 0; matrix products, arithmetic and copies ran while one was open for 0% -> 0% of each run, Pallas kernels for 0% -> 0%
where the time goes in v1:
time: 73.2 us; the launch traced here: 71.9 us
  Pallas kernels  65.4 us (89%)
  local copies, waits for them, and re-layouts  5.9 us (8%)
    pallas_call x1, Pallas kernels, body(): pl.pallas_call(kernel, out_shape=(jax.ShapeDtypeStruct((SHARE, PANEL), F3...  65.4 us
    unnamed x3, local copies, waits for them, and re-layouts  5.9 us

profile of v1, /device:TPU:8, one launch (start us, length us, event | category | flops | bytes accessed | tf_op | source)
XLA Modules:
  0.0 71.9 jit_solution(10811195419099625447)
XLA Ops:
  0.6 1.4 %copy.8.routes = s32[128,2]{1,0:T(8,128)} copy(s32[128,2]{0,1:T(2,128)} %param.7) | data formatting | bytes 2048 | tf_op args[1]
  2.0 65.4 %calibrate.1 = (f32[448,128]{1,0:T(8,128)}, bf16[128,7168]{1,0:T(8,128)(2,1)}) custom-call(bf16[128,7168]{1,0:T(8,128)(2,1)} %tokens.1, s32[128,2]{1,0:T(8,128)} %copy.8.routes, s32[16]{0:T(128)} %owner.1, bf16[128,7168]{1,0:T(8,128)(2,1)} %bitcast.7, f32[1,128]{1,0:T(1,128)} %hdiag.1, f32[128,7168]{1,0:T(8,128)} %bitcast.6), custom_call_target="tpu_custom_call" | custom-call | flops 4000000000 | bytes 10000000 | tf_op jit(solution)/shard_map/calibrate/pallas_call | solution.py:543
  67.4 1.6 %copy.11 = f32[1,448,128]{2,1,0:T(8,128)} copy(f32[1,448,128]{2,1,0:T(8,128)} %bitcast.5) | data formatting | bytes 458752
  69.1 2.8 %copy.12 = bf16[1,128,7168]{2,1,0:T(8,128)(2,1)} copy(bf16[1,128,7168]{2,1,0:T(8,128)(2,1)} %bitcast.4) | data formatting | bytes 3670016

commit v2 on v0

v2 whole, which is shorter than its diff:
```python
import math

import jax
import jax.numpy as jnp
from jax import lax
from jax.experimental import pallas as pl
from jax.experimental.pallas import tpu as pltpu
from jax.sharding import PartitionSpec as P

D = 7168
PANEL = 128
TOP = 2
TOK = 128
SLOTS = 16
RING = 8
PLANE = 16
SHARE = 448
MSG = PANEL + SLOTS
MESH = pl.DeviceIdType.MESH
BF16 = jnp.bfloat16
F32 = jnp.float32
SCALE = 16.0 / 65536.0

SINE = (
    6.2831852700170625,
    -16.20895564378196,
    16.769189671870134,
    -9.624604702175908,
    3.5163760294927235,
    -0.7983429889808796,
)


def sine_of_turns(turns):
    r = turns - jnp.round(turns)
    y = r * r
    y2 = y * y
    low = SINE[0] + SINE[1] * y
    mid = SINE[2] + SINE[3] * y
    top = SINE[4] + SINE[5] * y
    edge = r - 4.0 * (r * y)
    return edge * (low + y2 * (mid + y2 * top))


def place_of(x):
    return jnp.where(x == 0, 0, jnp.where(x == 3, 1, x + 1))


def kernel(
    tokens,
    routes,
    owner,
    weights,
    hdiag,
    hrows,
    gram,
    updated,
    x0,
    msg,
    w_v,
    h_v,
    dg_own,
    dg_in,
    dg_mid,
    dg_fin,
    mt,
    x_left,
    x_two,
    x_one,
    ht,
    rot,
    work,
    inv,
    amp,
    dinv,
    errs,
    sib_out,
    sib_in,
    own,
    z_out,
    z_in,
    hold,
    fin,
    left,
    left_out,
    left_in,
    local_sem,
    dg_s,
    dg_r,
    dgz_s,
    dgz_r,
    pm_s,
    pm_r,
    xl_s,
    xl_r,
    xm_s,
    xm_r,
    sib_s,
    sib_r,
    z_s,
    z_r,
    lx_s,
    lx_r,
):
    e = lax.axis_index("expert")
    t = lax.axis_index("token")
    z, c = e // 2, e % 2
    y, x = t // 4, t % 4
    place = place_of(x)
    u = 4 * place + y
    group = place // 2
    side = x % 2

    ys = [y] + [(y + k) % 4 for k in range(1, 4)]
    xs = [x, 3 - x, (x + 2) % 4, (5 - x) % 4]
    places = [place] + [place_of(px) for px in xs[1:]]
    plane = [(ys[k // 4], xs[k % 4], 4 * places[k % 4] + ys[k // 4]) for k in range(16)]
    others = plane[1:]
    near_first = [k for k in range(1, 16) if k % 4 < 2] + [k for k in range(1, 16) if k % 4 >= 2]
    half_ring = [plane[4 * (k // 2) + k % 2] for k in range(8)]
    experts = [(e + k) % 16 for k in range(1, 16)]

    def ring(steps):
        return (z + jnp.where(c == 0, steps % RING, -steps % RING)) % RING

    def tile_rows(index):
        return pl.ds(pl.multiple_of(index * TOK, TOK), TOK)

    def main_lanes(py, px, part):
        first = 7 * (2 * py + px // 2) + 4 * (px % 2) + 2 * part
        return pl.ds(pl.multiple_of(first * 128, 128), 256 - 128 * part)

    def stage_lanes(index):
        return (pl.ds(0, 128), pl.ds(128, 256), pl.ds(384, 128))[index]

    def left_lanes(py, px):
        return pl.ds(pl.multiple_of((7 * (2 * py + px // 2) + 3) * 128, 128), 128)

    def remote(src, dst, send, recv, device):
        return pltpu.make_async_remote_copy(
            src_ref=src,
            dst_ref=dst,
            send_sem=send,
            recv_sem=recv,
            device_id=device,
            device_id_type=MESH,
        )

    sent = []

    def start(copy):
        copy.start()
        sent.append(copy)

    barrier = pltpu.get_barrier_semaphore()
    for py, px, _ in others:
        pl.semaphore_signal(barrier, inc=1, device_id=(e, 4 * py + px), device_id_type=MESH)
    for pe in experts:
        pl.semaphore_signal(barrier, inc=1, device_id=(pe, t), device_id_type=MESH)

    get_x0 = pltpu.make_async_copy(tokens.at[:, pl.ds(0, 128)], x0, local_sem.at[0])
    get_w = pltpu.make_async_copy(weights, w_v, local_sem.at[1])
    get_h = pltpu.make_async_copy(hrows, h_v, local_sem.at[2])
    get_x0.start()
    get_w.start()
    get_h.start()

    first = jnp.broadcast_to(routes[0:1, :], (SLOTS, TOK))
    second = jnp.broadcast_to(routes[1:2, :], (SLOTS, TOK))
    slot_a = jnp.zeros((SLOTS, TOK), jnp.int32)
    slot_b = jnp.zeros((SLOTS, TOK), jnp.int32)
    for i in range(SLOTS):
        slot_a = jnp.where(first == i, owner[i], slot_a)
        slot_b = jnp.where(second == i, owner[i], slot_b)
    slot_row = lax.broadcasted_iota(jnp.int32, (SLOTS, TOK), 0)
    mask = jnp.where((slot_a == slot_row) | (slot_b == slot_row), 1.0, 0.0).astype(F32)

    get_x0.wait()
    panel = x0[...].astype(F32)
    square = panel * panel
    high = square.astype(BF16)
    low = (square - high.astype(F32)).astype(BF16)
    mask16 = mask.astype(BF16)
    dg_own[...] = jnp.dot(mask16, high, preferred_element_type=F32) + jnp.dot(
        mask16, low, preferred_element_type=F32
    )
    msg[pl.ds(u, 1), pl.ds(0, PANEL), :] = panel.T.astype(BF16)[None]
    msg[pl.ds(u, 1), pl.ds(PANEL, SLOTS), :] = mask16[None]

    pl.semaphore_wait(barrier, 30)

    for k, (py, px, _) in enumerate(others):
        start(remote(dg_own, dg_in.at[u], dg_s.at[k], dg_r.at[u], (e, 4 * py + px)))
    for k in near_first:
        py, px, _ = plane[k]
        start(remote(msg.at[u], msg.at[u], pm_s.at[k], pm_r.at[u], (e, 4 * py + px)))
    for k, (py, px, _) in enumerate(half_ring):
        src = tokens.at[:, left_lanes(py, px)]
        dst = x_left.at[tile_rows(u - 8 * group)]
        if k == 0:
            keep_left = pltpu.make_async_copy(src, dst, local_sem.at[3])
            keep_left.start()
        else:
            start(remote(src, dst, xl_s.at[k], xl_r.at[u - 8 * group], (e, 4 * py + px)))

    x_main = (x_two, x_one)
    keeps = []
    for part in range(2):
        keep = pltpu.make_async_copy(
            tokens.at[:, main_lanes(y, x, part)], x_main[part].at[tile_rows(u)], local_sem.at[4 + part]
        )
        keep.start()
        keeps.append(keep)
    dg_in[pl.ds(u, 1)] = dg_own[...][None]

    for part in range(2):
        for k, (py, px, _) in enumerate(others):
            src = tokens.at[:, main_lanes(py, px, part)]
            dst = x_main[part].at[tile_rows(u)]
            start(remote(src, dst, xm_s.at[part, k], xm_r.at[part, u], (e, 4 * py + px)))

    get_w.wait()
    get_h.wait()
    wide = w_v[:, 0:PANEL].astype(F32).T
    work[...] = wide
    step = jnp.max(jnp.abs(wide), axis=0, keepdims=True) / 7.0 + 1e-06
    cols = lax.broadcasted_iota(jnp.int32, (PANEL, PANEL), 0)
    rows = lax.broadcasted_iota(jnp.int32, (PANEL, PANEL), 1)
    ht[...] = jnp.where(cols > rows, h_v[:, 0:PANEL].T, 0.0)
    dinv[...] = 1.0 / jnp.broadcast_to(hdiag[...], (PANEL, PANEL)).T

    def mask_panel(sender):
        their = msg[sender, 0:PANEL, :]
        flags = msg[sender, PANEL:MSG, :]
        lanes = tile_rows(sender)
        for s in range(SLOTS):
            value = their * jnp.broadcast_to(flags[s : s + 1], (PANEL, TOK))
            at = jnp.where(c == s % 2, 1024, 0) + (s // 2) * PANEL
            mt[pl.ds(pl.multiple_of(at, PANEL), PANEL), lanes] = value

    def arrived_panels(column):
        @pl.loop(0, 4)
        def _(i):
            sender = 4 * places[column] + (y + i) % 4

            @pl.when(sender != u)
            def _():
                to = (e, 4 * ((y + i) % 4) + xs[column])
                remote(msg.at[sender], msg.at[sender], pm_s.at[0], pm_r.at[sender], to).wait_recv()

            mask_panel(sender)

    for k, (py, px, pu) in enumerate(others):
        remote(dg_own, dg_in.at[pu], dg_s.at[k], dg_r.at[pu], (e, 4 * py + px)).wait_recv()
    dg_mid[...] = jnp.sum(dg_in[...], axis=0)
    for k, pe in enumerate(experts):
        src = dg_mid.at[pl.ds(pl.multiple_of(8 * (pe // 8), 8), 8)]
        start(remote(src, dg_fin.at[e], dgz_s.at[k], dgz_r.at[e], (pe, t)))
    my_eight = pl.ds(pl.multiple_of(8 * (e // 8), 8), 8)
    dg_fin[pl.ds(e, 1)] = dg_mid[my_eight, :][None]

    arrived_panels(0)
    arrived_panels(1)

    def grams(index, source, is_left, meanwhile=lambda: None):
        lanes = stage_lanes(index)

        def product(first_row):
            if is_left:
                left_mt = mt[pl.ds(first_row, 1024), pl.ds(pl.multiple_of(group * 1024, 1024), 1024)]
                return jnp.dot(left_mt, source[...], preferred_element_type=F32)
            return jnp.dot(mt[pl.ds(first_row, 1024), :], source[...], preferred_element_type=F32)

        sib_out[:, lanes] = product(0).astype(BF16)
        swap = remote(
            sib_out.at[:, lanes],
            sib_in.at[:, lanes],
            sib_s.at[index],
            sib_r.at[index],
            (2 * z + 1 - c, t),
        )
        start(swap)
        own[:, lanes] = product(1024)
        meanwhile()
        swap.wait_recv()

        def block(steps):
            at = tile_rows(ring(steps))
            return own[at, lanes] + sib_in[at, lanes].astype(F32)

        for kind, (target, to) in enumerate(((-4, -2), (-3, -1), (3, 1), (-1, -1), (1, 1))):
            z_out[kind, :, lanes] = block(target).astype(BF16)
            start(z_copy(index, kind, to))
        hold[0, :, lanes] = block(-2)
        hold[1, :, lanes] = block(2)
        fin[:, lanes] = block(0)

    def z_copy(index, kind, steps):
        lanes = stage_lanes(index)
        return remote(
            z_out.at[kind, :, lanes],
            z_in.at[kind, :, lanes],
            z_s.at[index, kind],
            z_r.at[index, kind],
            (2 * ring(steps) + c, t),
        )

    def relay(index):
        lanes = stage_lanes(index)
        z_copy(index, 0, 2).wait_recv()
        z_copy(index, 1, 1).wait_recv()
        far = z_in[0, :, lanes].astype(F32) + z_in[1, :, lanes].astype(F32)
        z_out[5, :, lanes] = (hold[0, :, lanes] + far).astype(BF16)
        start(z_copy(index, 5, -2))
        z_copy(index, 2, -1).wait_recv()
        z_out[6, :, lanes] = (hold[1, :, lanes] + z_in[2, :, lanes].astype(F32)).astype(BF16)
        start(z_copy(index, 6, 2))

    def gather_sum(index):
        lanes = stage_lanes(index)
        acc = fin[:, lanes]
        for kind, steps in ((3, 1), (4, -1), (5, 2), (6, -2)):
            z_copy(index, kind, steps).wait_recv()
            acc = acc + z_in[kind, :, lanes].astype(F32)
        return acc.T * SCALE

    for k, pe in enumerate(experts):
        src = dg_mid.at[my_eight]
        remote(src, dg_fin.at[pe], dgz_s.at[k], dgz_r.at[pe], (pe, t)).wait_recv()
    eight = jnp.sum(dg_fin[...], axis=0)
    this = lax.broadcasted_iota(jnp.int32, (8, 128), 0) == e % 8
    dgram = jnp.sum(jnp.where(this, eight, 0.0), axis=0, keepdims=True) * SCALE
    colfac = jnp.sqrt(jnp.mean(dgram, axis=1, keepdims=True) / (dgram + 1e-05))
    grid_step = jnp.broadcast_to(colfac, (PANEL, PANEL)).T * step
    amp[...] = grid_step / (2.0 * math.pi)
    inv[...] = 1.0 / grid_step

    def round_columns(b):
        j0 = pl.multiple_of(b * 8, 8)
        at = pl.ds(j0, 8)
        rot[...] = pltpu.roll(ht[...], (PANEL - b * 8) % PANEL, 1)
        near = rot[at, :]
        block = work[at, :]
        inv_b, amp_b, dinv_b = inv[at, :], amp[at, :], dinv[at, :]
        row = lax.broadcasted_iota(jnp.int32, (8, 128), 0)
        faults = []
        fault_rows = jnp.zeros((8, 128), F32)
        for j in range(8):
            value = jnp.broadcast_to(block[j : j + 1], (8, 128))
            turns = value * jnp.broadcast_to(inv_b[j : j + 1], (8, 128))
            moved = sine_of_turns(turns) * jnp.broadcast_to(amp_b[j : j + 1], (8, 128))
            fault = moved * jnp.broadcast_to(dinv_b[j : j + 1], (8, 128))
            coef = jnp.broadcast_to(near[:, j : j + 1], (8, 128))
            block = jnp.where(row == j, value - moved, block - fault * coef)
            fault_rows = jnp.where(row == j, fault, fault_rows)
            faults.append(fault)
        for k in range(16):
            part = pl.ds(8 * k, 8)
            acc = work[part, :]
            for j in range(8):
                acc = acc - faults[j] * jnp.broadcast_to(rot[part, j : j + 1], (8, 128))
            work[part, :] = acc
        work[at, :] = block
        errs[at, :] = fault_rows

    @pl.loop(0, 16)
    def _(b):
        round_columns(b)

    def arrived_part(part):
        keeps[part].wait()
        for k, (py, px, pu) in enumerate(others):
            src = tokens.at[:, main_lanes(py, px, part)]
            dst = x_main[part].at[tile_rows(pu)]
            remote(src, dst, xm_s.at[part, k], xm_r.at[part, pu], (e, 4 * py + px)).wait_recv()

    arrived_panels(2)
    arrived_panels(3)

    for k, (py, px, pu) in enumerate(half_ring):
        if k == 0:
            keep_left.wait()
        else:
            src = tokens.at[:, left_lanes(py, px)]
            dst = x_left.at[tile_rows(pu - 8 * group)]
            remote(src, dst, xl_s.at[k], xl_r.at[pu - 8 * group], (e, 4 * py + px)).wait_recv()
    grams(0, x_left, True)


    err_rows = errs[...].T.astype(BF16)

    @pl.loop(0, 14)
    def _(i):
        lanes = pl.ds(pl.multiple_of(i * 512, 512), 512)
        fix = jnp.dot(err_rows, h_v[:, lanes].astype(BF16), preferred_element_type=F32)
        updated[:, lanes] = (w_v[:, lanes].astype(F32) - fix).astype(BF16)

    updated[:, 0:PANEL] = work[...].T.astype(BF16)
    relay(0)

    arrived_part(0)
    grams(1, x_two, False)

    left[...] = gather_sum(0)
    half_rows = pl.ds(pl.multiple_of((1 - side) * 64, 64), 64)
    left_out[...] = left[half_rows, :]
    swap_left = remote(left_out, left_in, lx_s.at[0], lx_r.at[0], (e, 4 * y + x + 1 - 2 * side))
    start(swap_left)

    arrived_part(1)
    grams(2, x_one, False, lambda: relay(1))

    base = 64 * side
    swap_left.wait_recv()
    left_at = pl.ds(pl.multiple_of(384 * (1 - side), 64), 64)
    gram[left_at, :] = left[pl.ds(pl.multiple_of(side * 64, 64), 64), :] + left_in[...]
    gram[pl.ds(pl.multiple_of(base, 64), 256), :] = gather_sum(1)
    relay(2)
    gram[pl.ds(pl.multiple_of(base + 256, 64), 128), :] = gather_sum(2)

    for copy in sent:
        copy.wait_send()


def body(tokens, routes, owner_of, weights, hinv_diag, hinv_rows):
    vmem = pl.BlockSpec(memory_space=pltpu.VMEM)
    hbm = pl.BlockSpec(memory_space=pl.ANY)
    dma = pltpu.SemaphoreType.DMA
    square = pltpu.VMEM((PANEL, PANEL), F32)
    gram, updated = pl.pallas_call(
        kernel,
        out_shape=(pltpu.VMEM((SHARE, PANEL), F32), pltpu.VMEM((128, D), BF16)),
        in_specs=[hbm, vmem, pl.BlockSpec(memory_space=pltpu.SMEM), hbm, vmem, hbm],
        out_specs=(vmem, vmem),
        scratch_shapes=[
            pltpu.VMEM((TOK, 128), BF16),
            pltpu.VMEM((PLANE, MSG, TOK), BF16),
            pltpu.VMEM((128, D), BF16),
            pltpu.VMEM((PANEL, D), F32),
            pltpu.VMEM((SLOTS, PANEL), F32),
            pltpu.VMEM((PLANE, SLOTS, PANEL), F32),
            pltpu.VMEM((SLOTS, PANEL), F32),
            pltpu.VMEM((16, 8, PANEL), F32),
            pltpu.VMEM((SLOTS * PANEL, PLANE * TOK), BF16),
            pltpu.VMEM((8 * TOK, 128), BF16),
            pltpu.VMEM((PLANE * TOK, 256), BF16),
            pltpu.VMEM((PLANE * TOK, 128), BF16),
            square,
            square,
            square,
            square,
            square,
            square,
            square,
            pltpu.VMEM((RING * PANEL, 512), BF16),
            pltpu.VMEM((RING * PANEL, 512), BF16),
            pltpu.VMEM((RING * PANEL, 512), F32),
            pltpu.VMEM((7, PANEL, 512), BF16),
            pltpu.VMEM((7, PANEL, 512), BF16),
            pltpu.VMEM((2, PANEL, 512), F32),
            pltpu.VMEM((PANEL, 512), F32),
            square,
            pltpu.VMEM((64, PANEL), F32),
            pltpu.VMEM((64, PANEL), F32),
            dma((8,)),
            dma((15,)),
            dma((16,)),
            dma((15,)),
            dma((16,)),
            dma((16,)),
            dma((16,)),
            dma((8,)),
            dma((8,)),
            dma((2, 15)),
            dma((2, 16)),
            dma((3,)),
            dma((3,)),
            dma((3, 7)),
            dma((3, 7)),
            dma((1,)),
            dma((1,)),
        ],
        compiler_params=pltpu.CompilerParams(
            collective_id=0, has_side_effects=True, vmem_limit_bytes=61 * 2**20
        ),
        cost_estimate=pl.CostEstimate(flops=4 * 10**9, bytes_accessed=10**7, transcendentals=0),
        name="calibrate",
    )(tokens, routes.T, owner_of, weights[0], hinv_diag, hinv_rows[0])
    return gram[None], updated[None]


def solution(mesh):
    in_specs = (
        P(("expert", "token"), None),
        P(("expert", "token"), None),
        P(),
        P("expert", "token", None),
        P("expert", None),
        P("expert", None, None),
    )
    out_specs = (P("expert", "token", None), P("expert", "token", None))
    return jax.shard_map(body, mesh=mesh, in_specs=in_specs, out_specs=out_specs, check_vma=False)
```

time: 605 us -> 65.2 us (0.11); the launches traced: 598 us -> 65.1 us
  other arithmetic: 204 us -> 0 us
  blocking collectives: 170 us -> 0 us
  waiting for transfers between devices: 103 us -> 0 us
  local copies, waits for them, and re-layouts: 89.5 us -> 1.92 us
  Pallas kernels: 0 us -> 62.5 us
  between operations: 14.8 us -> 0.64 us
  matrix products: 11.7 us -> 0 us
    mul x257 -> x0, other arithmetic: 179 us -> none  [the longest x256 179 us: advance(): panel = panel - fault[:, None] * row[None, :]]
    all_to_all x1 -> x0, blocking collectives: 170 us -> none  [body(): lax.all_to_all(send, 'expert', split_axis=0, concat_axis=0, tiled=True)]
    psum x1 -> x0, waiting for transfers between devices: 103 us -> none  [body(): total = lax.psum(partial_sum, 'token')]
    dynamic_slice x128 -> x0, local copies, waits for them, and re-layouts: 75 us -> none  [advance(): fault = (value - rounded) / diag_block[j]]
    pallas_call x0 -> x1, Pallas kernels: none -> 62.5 us  [body(): pl.pallas_call(kernel, out_shape=(pltpu.VMEM((SHARE, PANEL), F32), pltpu....]
    select_n x130 -> x0, other arithmetic: 17.6 us -> none  [the longest x128 13.9 us: advance(): errors = jnp.where(column_ids[None, :] == j, fault[:, None], errors)]
    dot_general x2 -> x0, matrix products: 11.7 us -> none  [the longest x1 7.69 us: round_panel(): jnp.dot(errors, factor_rows[:, PANEL:], precision=lax.Precision.HIGHEST)]
    gather x2 -> x0, local copies, waits for them, and re-layouts: 8.29 us -> none  [the longest x1 7.05 us: body(): tokens[source]]
  transfers between devices with their start and end apart: 1 -> 0, of which waited for: 1 -> 0; matrix products, arithmetic and copies ran while one was open for 0% -> 0% of each run, Pallas kernels for 0% -> 0%
where the time goes in v2:
time: 65.2 us; the launch traced here: 65.1 us
  Pallas kernels  62.5 us (96%)
  local copies, waits for them, and re-layouts  1.92 us (3%)
    pallas_call x1, Pallas kernels, body(): pl.pallas_call(kernel, out_shape=(pltpu.VMEM((SHARE, PANEL), F32), pltpu....  62.5 us
    unnamed x2, local copies, waits for them, and re-layouts  1.92 us

profile of v2, /device:TPU:8, one launch (start us, length us, event | category | flops | bytes accessed | tf_op | source)
XLA Modules:
  0.0 65.1 jit_solution(14743206341354494951)
XLA Ops:
  0.6 62.5 %calibrate.1 = (f32[448,128]{1,0:T(8,128)S(1)}, bf16[128,7168]{1,0:T(8,128)(2,1)S(1)}) custom-call(bf16[128,7168]{1,0:T(8,128)(2,1)} %tokens.1, s32[2,128]{1,0:T(2,128)} %bitcast.9, s32[16]{0:T(128)} %owner.1, bf16[128,7168]{1,0:T(8,128)(2,1)} %bitcast.8, f32[1,128]{1,0:T(1,128)} %hdiag.1, f32[128,7168]{1,0:T(8,128)} %bitcast.7), custom_call_target="tpu_custom_call" | custom-call | flops 4000000000 | bytes 10000000 | tf_op jit(solution)/shard_map/calibrate/pallas_call | solution.py:430
  63.2 0.7 %copy.10 = f32[1,448,128]{2,1,0:T(8,128)} copy(f32[1,448,128]{2,1,0:T(8,128)S(1)} %bitcast.6) | data formatting | bytes 458752
  63.8 1.2 %copy.11 = bf16[1,128,7168]{2,1,0:T(8,128)(2,1)} copy(bf16[1,128,7168]{2,1,0:T(8,128)(2,1)S(1)} %bitcast.5) | data formatting | bytes 3670016

commit v3 on v2

--- a/solution.py
+++ b/solution.py
@@ -42,23 +42,30 @@
     return edge * (low + y2 * (mid + y2 * top))
 
 
+DIRECT = (4, 3, -3, 2, -2, 1, -1)
+
+
 def place_of(x):
     return jnp.where(x == 0, 0, jnp.where(x == 3, 1, x + 1))
 
 
 def kernel(
     tokens,
-    routes,
-    owner,
+    routes_in,
+    owner_in,
     weights,
-    hdiag,
+    hdiag_in,
     hrows,
     gram,
     updated,
+    routes,
+    owner,
+    hdiag,
     x0,
     msg,
     w_v,
     h_v,
+    h_half,
     dg_own,
     dg_in,
     dg_mid,
@@ -91,6 +98,8 @@
     dgz_r,
     pm_s,
     pm_r,
+    pc_s,
+    pc_r,
     xl_s,
     xl_r,
     xm_s,
@@ -116,7 +125,6 @@
     places = [place] + [place_of(px) for px in xs[1:]]
     plane = [(ys[k // 4], xs[k % 4], 4 * places[k % 4] + ys[k // 4]) for k in range(16)]
     others = plane[1:]
-    near_first = [k for k in range(1, 16) if k % 4 < 2] + [k for k in range(1, 16) if k % 4 >= 2]
     half_ring = [plane[4 * (k // 2) + k % 2] for k in range(8)]
     experts = [(e + k) % 16 for k in range(1, 16)]
 
@@ -161,10 +169,19 @@
     get_x0 = pltpu.make_async_copy(tokens.at[:, pl.ds(0, 128)], x0, local_sem.at[0])
     get_w = pltpu.make_async_copy(weights, w_v, local_sem.at[1])
     get_h = pltpu.make_async_copy(hrows, h_v, local_sem.at[2])
+    get_small = [
+        pltpu.make_async_copy(routes_in, routes, local_sem.at[8]),
+        pltpu.make_async_copy(owner_in, owner, local_sem.at[9]),
+        pltpu.make_async_copy(hdiag_in, hdiag, local_sem.at[10]),
+    ]
+    for copy in get_small:
+        copy.start()
     get_x0.start()
     get_w.start()
     get_h.start()
 
+    for copy in get_small:
+        copy.wait()
     first = jnp.broadcast_to(routes[0:1, :], (SLOTS, TOK))
     second = jnp.broadcast_to(routes[1:2, :], (SLOTS, TOK))
     slot_a = jnp.zeros((SLOTS, TOK), jnp.int32)
@@ -191,8 +208,8 @@
 
     for k, (py, px, _) in enumerate(others):
         start(remote(dg_own, dg_in.at[u], dg_s.at[k], dg_r.at[u], (e, 4 * py + px)))
-    for k in near_first:
-        py, px, _ = plane[k]
+    for k in range(1, 8):
+        py, px, _ = half_ring[k]
         start(remote(msg.at[u], msg.at[u], pm_s.at[k], pm_r.at[u], (e, 4 * py + px)))
     for k, (py, px, _) in enumerate(half_ring):
         src = tokens.at[:, left_lanes(py, px)]
@@ -213,11 +230,19 @@
         keeps.append(keep)
     dg_in[pl.ds(u, 1)] = dg_own[...][None]
 
-    for part in range(2):
+    for k in range(1, 4):
+        pu = 4 * place + ys[k]
+        remote(msg.at[pu], msg.at[pu], pm_s.at[0], pm_r.at[pu], (e, 4 * ys[k] + x)).wait_recv()
+    column = pl.ds(4 * place, 4)
+    for k in (2, 3):
+        start(remote(msg.at[column], msg.at[column], pc_s.at[k], pc_r.at[x], (e, 4 * y + xs[k])))
+    def send_part(part):
         for k, (py, px, _) in enumerate(others):
             src = tokens.at[:, main_lanes(py, px, part)]
             dst = x_main[part].at[tile_rows(u)]
             start(remote(src, dst, xm_s.at[part, k], xm_r.at[part, u], (e, 4 * py + px)))
+
+    send_part(0)
 
     get_w.wait()
     get_h.wait()
@@ -229,6 +254,12 @@
     ht[...] = jnp.where(cols > rows, h_v[:, 0:PANEL].T, 0.0)
     dinv[...] = 1.0 / jnp.broadcast_to(hdiag[...], (PANEL, PANEL)).T
 
+    @pl.loop(0, 14)
+    def _(i):
+        lanes = pl.ds(pl.multiple_of(i * 512, 512), 512)
+        h_half[:, lanes] = h_v[:, lanes].astype(BF16)
+
+
     def mask_panel(sender):
         their = msg[sender, 0:PANEL, :]
         flags = msg[sender, PANEL:MSG, :]
@@ -239,16 +270,18 @@
             mt[pl.ds(pl.multiple_of(at, PANEL), PANEL), lanes] = value
 
     def arrived_panels(column):
+        if column == 1:
+            for k in range(4):
+                pu = 4 * places[1] + ys[k]
+                remote(msg.at[pu], msg.at[pu], pm_s.at[0], pm_r.at[pu], (e, 4 * ys[k] + xs[1])).wait_recv()
+        if column > 1:
+            theirs = pl.ds(4 * places[column], 4)
+            px = xs[column]
+            remote(msg.at[theirs], msg.at[theirs], pc_s.at[column], pc_r.at[px], (e, 4 * y + px)).wait_recv()
+
         @pl.loop(0, 4)
         def _(i):
-            sender = 4 * places[column] + (y + i) % 4
-
-            @pl.when(sender != u)
-            def _():
-                to = (e, 4 * ((y + i) % 4) + xs[column])
-                remote(msg.at[sender], msg.at[sender], pm_s.at[0], pm_r.at[sender], to).wait_recv()
-
-            mask_panel(sender)
+            mask_panel(4 * places[column] + i)
 
     for k, (py, px, pu) in enumerate(others):
         remote(dg_own, dg_in.at[pu], dg_s.at[k], dg_r.at[pu], (e, 4 * py + px)).wait_recv()
@@ -281,12 +314,19 @@
         )
         start(swap)
         own[:, lanes] = product(1024)
-        meanwhile()
+        result = meanwhile()
         swap.wait_recv()
 
         def block(steps):
             at = tile_rows(ring(steps))
             return own[at, lanes] + sib_in[at, lanes].astype(F32)
+
+        if index == 2:
+            for kind, steps in enumerate(DIRECT):
+                z_out[kind, :, lanes] = block(steps).astype(BF16)
+                start(z_copy(index, kind, steps))
+            fin[:, lanes] = block(0)
+            return result
 
         for kind, (target, to) in enumerate(((-4, -2), (-3, -1), (3, 1), (-1, -1), (1, 1))):
             z_out[kind, :, lanes] = block(target).astype(BF16)
@@ -294,6 +334,7 @@
         hold[0, :, lanes] = block(-2)
         hold[1, :, lanes] = block(2)
         fin[:, lanes] = block(0)
+        return result
 
     def z_copy(index, kind, steps):
         lanes = stage_lanes(index)
@@ -319,7 +360,10 @@
     def gather_sum(index):
         lanes = stage_lanes(index)
         acc = fin[:, lanes]
-        for kind, steps in ((3, 1), (4, -1), (5, 2), (6, -2)):
+        arriving = ((3, 1), (4, -1), (5, 2), (6, -2))
+        if index == 2:
+            arriving = [(kind, -steps) for kind, steps in enumerate(DIRECT)]
+        for kind, steps in arriving:
             z_copy(index, kind, steps).wait_recv()
             acc = acc + z_in[kind, :, lanes].astype(F32)
         return acc.T * SCALE
@@ -377,6 +421,8 @@
     arrived_panels(2)
     arrived_panels(3)
 
+    send_part(1)
+
     for k, (py, px, pu) in enumerate(half_ring):
         if k == 0:
             keep_left.wait()
@@ -392,20 +438,22 @@
     @pl.loop(0, 14)
     def _(i):
         lanes = pl.ds(pl.multiple_of(i * 512, 512), 512)
-        fix = jnp.dot(err_rows, h_v[:, lanes].astype(BF16), preferred_element_type=F32)
+        fix = jnp.dot(err_rows, h_half[:, lanes], preferred_element_type=F32)
         updated[:, lanes] = (w_v[:, lanes].astype(F32) - fix).astype(BF16)
 
     updated[:, 0:PANEL] = work[...].T.astype(BF16)
     relay(0)
 
     arrived_part(0)
-    grams(1, x_two, False)
-
-    left[...] = gather_sum(0)
-    half_rows = pl.ds(pl.multiple_of((1 - side) * 64, 64), 64)
-    left_out[...] = left[half_rows, :]
-    swap_left = remote(left_out, left_in, lx_s.at[0], lx_r.at[0], (e, 4 * y + x + 1 - 2 * side))
-    start(swap_left)
+    def end_left():
+        left[...] = gather_sum(0)
+        half_rows = pl.ds(pl.multiple_of((1 - side) * 64, 64), 64)
+        left_out[...] = left[half_rows, :]
+        swap_left = remote(left_out, left_in, lx_s.at[0], lx_r.at[0], (e, 4 * y + x + 1 - 2 * side))
+        start(swap_left)
+        return swap_left
+
+    swap_left = grams(1, x_two, False, end_left)
 
     arrived_part(1)
     grams(2, x_one, False, lambda: relay(1))
@@ -415,11 +463,21 @@
     left_at = pl.ds(pl.multiple_of(384 * (1 - side), 64), 64)
     gram[left_at, :] = left[pl.ds(pl.multiple_of(side * 64, 64), 64), :] + left_in[...]
     gram[pl.ds(pl.multiple_of(base, 64), 256), :] = gather_sum(1)
-    relay(2)
     gram[pl.ds(pl.multiple_of(base + 256, 64), 128), :] = gather_sum(2)
 
     for copy in sent:
         copy.wait_send()
+
+
+def hand_over(gram_in, updated_in, gram, updated, sem):
+    copies = [pltpu.make_async_copy(gram_in, gram, sem.at[8])]
+    for i in range(8):
+        at = pl.ds(16 * i, 16)
+        copies.append(pltpu.make_async_copy(updated_in.at[at], updated.at[at], sem.at[i]))
+    for copy in copies:
+        copy.start()
+    for copy in copies:
+        copy.wait()
 
 
 def body(tokens, routes, owner_of, weights, hinv_diag, hinv_rows):
@@ -430,13 +488,17 @@
     gram, updated = pl.pallas_call(
         kernel,
         out_shape=(pltpu.VMEM((SHARE, PANEL), F32), pltpu.VMEM((128, D), BF16)),
-        in_specs=[hbm, vmem, pl.BlockSpec(memory_space=pltpu.SMEM), hbm, vmem, hbm],
+        in_specs=[hbm] * 6,
         out_specs=(vmem, vmem),
         scratch_shapes=[
+            pltpu.VMEM((TOP, TOK), jnp.int32),
+            pltpu.SMEM((SLOTS,), jnp.int32),
+            pltpu.VMEM((1, PANEL), F32),
             pltpu.VMEM((TOK, 128), BF16),
             pltpu.VMEM((PLANE, MSG, TOK), BF16),
             pltpu.VMEM((128, D), BF16),
             pltpu.VMEM((PANEL, D), F32),
+            pltpu.VMEM((PANEL, D), BF16),
             pltpu.VMEM((SLOTS, PANEL), F32),
             pltpu.VMEM((PLANE, SLOTS, PANEL), F32),
             pltpu.VMEM((SLOTS, PANEL), F32),
@@ -462,13 +524,15 @@
             square,
             pltpu.VMEM((64, PANEL), F32),
             pltpu.VMEM((64, PANEL), F32),
-            dma((8,)),
+            dma((11,)),
             dma((15,)),
             dma((16,)),
             dma((15,)),
             dma((16,)),
             dma((16,)),
             dma((16,)),
+            dma((4,)),
+            dma((4,)),
             dma((8,)),
             dma((8,)),
             dma((2, 15)),
@@ -486,6 +550,20 @@
         cost_estimate=pl.CostEstimate(flops=4 * 10**9, bytes_accessed=10**7, transcendentals=0),
         name="calibrate",
     )(tokens, routes.T, owner_of, weights[0], hinv_diag, hinv_rows[0])
+    gram, updated = pl.pallas_call(
+        hand_over,
+        out_shape=(
+            jax.ShapeDtypeStruct((SHARE, PANEL), F32),
+            jax.ShapeDtypeStruct((128, D), BF16),
+        ),
+        in_specs=[vmem, vmem],
+        out_specs=(hbm, hbm),
+        scratch_shapes=[dma((9,))],
+        name="hand_over",
+    )(
+        pltpu.with_memory_space_constraint(gram, pltpu.VMEM),
+        pltpu.with_memory_space_constraint(updated, pltpu.VMEM),
+    )
     return gram[None], updated[None]
 
 

time: 65.2 us -> 62 us (0.951)
  local copies, waits for them, and re-layouts: 1.92 us -> 0 us
  Pallas kernels: 62.5 us -> 61.2 us
    pallas_call x1, Pallas kernels: 62.5 us -> 59.9 us  [body(): pl.pallas_call(kernel, out_shape=(pltpu.VMEM((SHARE, PANEL), F32), pltpu....]
    unnamed x2 -> x0, local copies, waits for them, and re-layouts: 1.92 us -> none
    pallas_call x0 -> x1, Pallas kernels: none -> 1.37 us  [body(): pl.pallas_call(hand_over, out_shape=(jax.ShapeDtypeStruct((SHARE, PANEL),...]
where the time goes in v3:
time: 62 us; the launch traced here: 61.9 us
  Pallas kernels  61.2 us (99%)
  between operations  0.64 us (1%)
    pallas_call x1, Pallas kernels, body(): pl.pallas_call(kernel, out_shape=(pltpu.VMEM((SHARE, PANEL), F32), pltpu....  59.9 us
    pallas_call x1, Pallas kernels, body(): pl.pallas_call(hand_over, out_shape=(jax.ShapeDtypeStruct((SHARE, PANEL),...  1.37 us

profile of v3, /device:TPU:8, one launch (start us, length us, event | category | flops | bytes accessed | tf_op | source)
XLA Modules:
  0.0 61.9 jit_solution(8868181737221403013)
XLA Ops:
  0.6 59.9 %calibrate.1 = (f32[448,128]{1,0:T(8,128)S(1)}, bf16[128,7168]{1,0:T(8,128)(2,1)S(1)}) custom-call(bf16[128,7168]{1,0:T(8,128)(2,1)} %tokens.1, s32[2,128]{1,0:T(2,128)} %bitcast.9, s32[16]{0:T(128)} %owner_in.1, bf16[128,7168]{1,0:T(8,128)(2,1)} %bitcast.6, f32[1,128]{1,0:T(1,128)} %hdiag_in.1, f32[128,7168]{1,0:T(8,128)} %bitcast.5), custom_call_target="tpu_custom_call" | custom-call | flops 4000000000 | bytes 10000000 | tf_op jit(solution)/shard_map/calibrate/pallas_call | solution.py:488
  60.5 1.4 %hand_over.1 = (f32[448,128]{1,0:T(8,128)}, bf16[128,7168]{1,0:T(8,128)(2,1)}) custom-call(f32[448,128]{1,0:T(8,128)S(1)} %get-tuple-element.6.gram_in, bf16[128,7168]{1,0:T(8,128)(2,1)S(1)} %get-tuple-element.7.updated_in), custom_call_target="tpu_custom_call" | custom-call | tf_op jit(solution)/shard_map/hand_over/pallas_call | solution.py:553

commit v4 on v3

--- a/solution.py
+++ b/solution.py
@@ -161,10 +161,10 @@
         sent.append(copy)
 
     barrier = pltpu.get_barrier_semaphore()
+    for pe in experts:
+        pl.semaphore_signal(barrier, inc=1, device_id=(pe, t), device_id_type=MESH)
     for py, px, _ in others:
         pl.semaphore_signal(barrier, inc=1, device_id=(e, 4 * py + px), device_id_type=MESH)
-    for pe in experts:
-        pl.semaphore_signal(barrier, inc=1, device_id=(pe, t), device_id_type=MESH)
 
     get_x0 = pltpu.make_async_copy(tokens.at[:, pl.ds(0, 128)], x0, local_sem.at[0])
     get_w = pltpu.make_async_copy(weights, w_v, local_sem.at[1])
@@ -379,7 +379,7 @@
     amp[...] = grid_step / (2.0 * math.pi)
     inv[...] = 1.0 / grid_step
 
-    def round_columns(b):
+    def round_columns(b, first):
         j0 = pl.multiple_of(b * 8, 8)
         at = pl.ds(j0, 8)
         rot[...] = pltpu.roll(ht[...], (PANEL - b * 8) % PANEL, 1)
@@ -398,18 +398,24 @@
             block = jnp.where(row == j, value - moved, block - fault * coef)
             fault_rows = jnp.where(row == j, fault, fault_rows)
             faults.append(fault)
-        for k in range(16):
+
+        def pass_on(k):
             part = pl.ds(8 * k, 8)
             acc = work[part, :]
             for j in range(8):
                 acc = acc - faults[j] * jnp.broadcast_to(rot[part, j : j + 1], (8, 128))
             work[part, :] = acc
+
+        for k in range(first, 16):
+            pass_on(k)
         work[at, :] = block
         errs[at, :] = fault_rows
 
-    @pl.loop(0, 16)
-    def _(b):
-        round_columns(b)
+    for quarter in range(4):
+
+        @pl.loop(4 * quarter, 4 * quarter + 4)
+        def _(b):
+            round_columns(b, 4 * quarter)
 
     def arrived_part(part):
         keeps[part].wait()

time: 62 us -> 62.4 us (level)
  no operation moved by 1% of the time
where the time goes in v4:
time: 62.4 us; the launch traced here: 62.2 us
  Pallas kernels  61.6 us (99%)
  between operations  0.64 us (1%)
    pallas_call x1, Pallas kernels, body(): pl.pallas_call(kernel, out_shape=(pltpu.VMEM((SHARE, PANEL), F32), pltpu....  60.2 us
    pallas_call x1, Pallas kernels, body(): pl.pallas_call(hand_over, out_shape=(jax.ShapeDtypeStruct((SHARE, PANEL),...  1.37 us

profile of v4, /device:TPU:8, one launch (start us, length us, event | category | flops | bytes accessed | tf_op | source)
XLA Modules:
  0.0 62.2 jit_solution(14691433843065401487)
XLA Ops:
  0.6 60.2 %calibrate.1 = (f32[448,128]{1,0:T(8,128)S(1)}, bf16[128,7168]{1,0:T(8,128)(2,1)S(1)}) custom-call(bf16[128,7168]{1,0:T(8,128)(2,1)} %tokens.1, s32[2,128]{1,0:T(2,128)} %bitcast.9, s32[16]{0:T(128)} %owner_in.1, bf16[128,7168]{1,0:T(8,128)(2,1)} %bitcast.6, f32[1,128]{1,0:T(1,128)} %hdiag_in.1, f32[128,7168]{1,0:T(8,128)} %bitcast.5), custom_call_target="tpu_custom_call" | custom-call | flops 4000000000 | bytes 10000000 | tf_op jit(solution)/shard_map/calibrate/pallas_call | solution.py:494
  60.9 1.4 %hand_over.1 = (f32[448,128]{1,0:T(8,128)}, bf16[128,7168]{1,0:T(8,128)(2,1)}) custom-call(f32[448,128]{1,0:T(8,128)S(1)} %get-tuple-element.6.gram_in, bf16[128,7168]{1,0:T(8,128)(2,1)S(1)} %get-tuple-element.7.updated_in), custom_call_target="tpu_custom_call" | custom-call | tf_op jit(solution)/shard_map/hand_over/pallas_call | solution.py:559
